TPU v7x, 256 devices: a whole 4x4x8 slice. The times are simulated.
256 devices in a mesh: pb: 16 (over y_hi, x, core), ka: 16 (over y_lo, z).
Axes of the slice: x: 4, y: 4 (y_hi: 2, y_lo: 2; y = y_hi * 2 + y_lo), z: 8, core: 2. Of those that a mesh axis runs over, the one named last changes fastest.
Arguments:
- queries: bfloat16 [32768, 1024], P(('pb', 'ka')), may hold values from -200 to 200
- keys: bfloat16 [32768, 128], P(('pb', 'ka')), may hold values from -6 to 6
- values: bfloat16 [32768, 128], P(('pb', 'ka')), may hold values from -6 to 6
- positions: int32 [32768], replicated, may hold values from 0 to 32767, as said below
Outputs:
- attended: float32 [32768, 1024], P(('pb', 'ka'))
Inputs may be any that keep to these rules, and one draw needn't show every extreme that they name: A permutation of 0 to 32767; each aligned run of 128 slots holds consecutive positions in increasing order.
All inputs are finite; a program needn't handle non-finite values.
Results may differ from a plain program's by a relative error of at most 0.0003.
Values may be sent and summed in bfloat16 or wider, within the bound.
A program may use at most 64 MiB of HBM per device.

v0:
```python
import math

import jax
import jax.numpy as jnp
from jax import lax
from jax.sharding import Mesh
from jax.sharding import PartitionSpec as P

HD = 128
KA = ("ka_0", "ka_1")
PB_KA = ("pb", "ka_0", "ka_1")


negative_big = -1e30


def laid_out(blocks, dim):
    shape = list(blocks.shape[1:])
    shape[dim] *= blocks.shape[0]
    return jnp.moveaxis(blocks, 0, dim).reshape(shape)


def all_blocks(array, axes, order):
    blocks = array[None]
    for k in order:
        blocks = lax.all_gather(blocks, axes[k], axis=0, tiled=True)
    current = [lax.axis_size(axes[k]) for k in reversed(order)]
    blocks = blocks.reshape(*current, *array.shape)
    turned = sorted(range(len(order)), key=lambda place: order[len(order) - 1 - place])
    return blocks.transpose(*turned, *range(len(order), blocks.ndim)).reshape(-1, *array.shape)


def whole_of(array, axes, order, dim):
    return laid_out(all_blocks(array, axes, order), dim)


def from_everyone(array, axis):
    peers = lax.axis_size(axis)
    return lax.all_to_all(
        jnp.broadcast_to(array[None], (peers, *array.shape)), axis, 0, 0, tiled=True
    )


def gather_directly(array, axis, dim):
    blocks = from_everyone(array, axis)
    return laid_out(blocks, dim)


def in_one_piece(arrays, axis, dim, along):
    widths = [a.shape[along] for a in arrays]
    both = jnp.concatenate(arrays, axis=along)
    whole = gather_directly(both, axis, dim)
    return tuple(jnp.split(whole, [sum(widths[:k]) for k in range(1, len(widths))], axis=along))


def side_by_side(arrays, axis, split_dim, concat_dim, along):
    widths = [math.prod(a.shape[along:]) for a in arrays]
    both = jnp.concatenate(
        [a.reshape(*a.shape[:along], w) for a, w in zip(arrays, widths)], axis=along
    )
    whole = lax.all_to_all(both, axis, split_axis=split_dim, concat_axis=concat_dim, tiled=True)
    blocks = jnp.split(whole, [sum(widths[:k]) for k in range(1, len(widths))], axis=along)
    return tuple(
        (b.reshape(*whole.shape[:along], *a.shape[along:]) for a, b in zip(arrays, blocks))
    )


def tile_update(state, rows, row_pos, key_rows, value_rows, key_pos):
    largest, totals, summed = state
    count = rows.shape[0]
    heads = rows.shape[1] // HD
    scale = 1.0 / HD**0.5
    grouped = rows.reshape(count, heads, HD)
    score = jnp.einsum("qhd,kd->hqk", grouped, key_rows, preferred_element_type=jnp.float32) * scale
    visible = (key_pos[None, :] <= row_pos[:, None])[None, :, :]
    masked = jnp.where(visible, score, negative_big)
    top = jnp.maximum(largest, jnp.max(masked, axis=2))
    weight = jnp.where(visible, jnp.exp(masked - top[:, :, None]), 0.0)
    factor = jnp.exp(largest - top)
    totals = totals * factor + jnp.sum(weight, axis=2)
    summed = summed * factor[:, :, None] + jnp.einsum(
        "hqk,kd->hqd", weight, value_rows.astype(jnp.float32), precision=lax.Precision.HIGHEST
    )
    return (top, totals, summed)


def empty_state(heads, count):
    return (
        jnp.full((heads, count), negative_big, jnp.float32),
        jnp.zeros((heads, count), jnp.float32),
        jnp.zeros((heads, count, HD), jnp.float32),
    )


def finish(summed, totals):
    heads, count, width = summed.shape
    output = summed / totals[:, :, None]
    return jnp.transpose(output, (1, 0, 2)).reshape(count, heads * width)


def local_partials(queries, keys, values, positions):
    own_count = queries.shape[0]
    heads = queries.shape[1] // HD
    size_query = lax.axis_size("pb")
    size_key = lax.axis_size(KA)
    index_query = lax.axis_index("pb")
    index_key = lax.axis_index(KA)
    block_rows = whole_of(queries, KA, (0, 1), 0)
    key_rows, value_rows = in_one_piece((keys, values), "pb", 0, 1)
    block_count = size_key * own_count
    block_pos = lax.dynamic_slice_in_dim(positions, index_query * block_count, block_count, 0)
    key_pos = lax.dynamic_slice_in_dim(
        positions.reshape(size_query, size_key, own_count), index_key, 1, 1
    ).reshape(-1)

    def query_run(run):
        rows = lax.dynamic_slice_in_dim(block_rows, run * own_count, own_count, 0)
        run_pos = lax.dynamic_slice_in_dim(block_pos, run * own_count, own_count, 0)
        run_end = run_pos[own_count - 1]

        def key_run(index, state):
            offset = index * own_count
            piece_pos = lax.dynamic_slice_in_dim(key_pos, offset, own_count, 0)
            piece_keys = lax.dynamic_slice_in_dim(key_rows, offset, own_count, 0)
            piece_values = lax.dynamic_slice_in_dim(value_rows, offset, own_count, 0)
            return lax.cond(
                piece_pos[0] <= run_end,
                lambda inner: tile_update(
                    inner, rows, run_pos, piece_keys, piece_values, piece_pos
                ),
                lambda inner: inner,
                state,
            )

        return lax.fori_loop(0, size_query, key_run, empty_state(heads, own_count))

    return lax.map(query_run, jnp.arange(size_key, dtype=jnp.int32))


def on_device(queries, keys, values, positions):
    largest, totals, summed = local_partials(queries, keys, values, positions)
    every_max, every_total, every_sum = side_by_side((largest, totals, summed), KA, 0, 0, 3)
    top = jnp.max(every_max, axis=0)
    factor = jnp.exp(every_max - top[None, :, :])
    merged_total = jnp.sum(every_total * factor, axis=0)
    merged_sum = jnp.sum(every_sum * factor[:, :, :, None], axis=0)
    return finish(merged_sum, merged_total)


def solution(mesh):
    finer = Mesh(mesh.devices.reshape(mesh.shape["pb"], 2, 8), ("pb", "ka_0", "ka_1"))
    placed = (P(PB_KA, None), P(PB_KA, None), P(PB_KA, None), P())
    return jax.shard_map(
        on_device, mesh=finer, in_specs=placed, out_specs=P(PB_KA, None), check_vma=False
    )
```

profile of v0, /device:TPU:19, one launch (start us, length us, event | category | flops | bytes accessed | tf_op | source)
XLA Modules:
  0.0 764.6 jit_solution(9676022444290708172)
XLA Ops:
  6.5 9.7 %all-gather = bf16[256,1024]{1,0:T(8,128)(2,1)} all-gather(bf16[128,1024]{1,0:T(8,128)(2,1)} %param.10), channel_id=2, replica_groups=mesh['pb'=16,'ka_0'=2,'ka_1'=8] {'ka_0'}, dimensions={0}, use_global_device_ids=true | all-gather | bytes 786432 | tf_op jit(solution)/shard_map/all_gather | solution.py:26
  18.2 8.1 %all-to-all-start = ((bf16[16,128,256]{2,1,0:T(8,128)(2,1)}), bf16[16,128,256]{2,1,0:T(8,128)(2,1)S(1)}, u32[]{:S(2)}, u32[]{:S(2)}) async-start(bf16[16,128,256]{2,1,0:T(8,128)(2,1)} %broadcast_in_dim.58), calls=%async_computation | async-start | bytes 2097152 | tf_op jit(solution)/shard_map/all_to_all | solution.py:39
  27.9 12.4 %all-to-all-done = bf16[16,128,256]{2,1,0:T(8,128)(2,1)S(1)} async-done(((bf16[16,128,256]{2,1,0:T(8,128)(2,1)}), bf16[16,128,256]{2,1,0:T(8,128)(2,1)S(1)}, u32[]{:S(2)}, u32[]{:S(2)}) %all-to-all-start) | async-done | bytes 1048608 | tf_op jit(solution)/shard_map/all_to_all | solution.py:39
  40.4 34.2 %all-gather.3.cloned.1.call-done = bf16[16,128,1024]{2,1,0:T(8,128)(2,1)} async-done(((bf16[2,128,1024]{2,1,0:T(8,128)(2,1)}), bf16[16,128,1024]{2,1,0:T(8,128)(2,1)}) %all-gather.3.cloned.1.call-update) | async-done | bytes 4194320 | tf_op jit(solution)/shard_map/all_gather | solution.py:26
  74.5 4.8 copy.26
  79.3 482.8 %while.32 = (s32[]{:T(128)}, f32[16,8,128]{2,1,0:T(8,128)S(1)}, f32[16,8,128]{2,1,0:T(8,128)S(1)}, f32[16,8,128,128]{2,1,3,0:T(8,128)}, s32[16]{0:T(128)S(1)}, /...) while((s32[]{:T(128)}, f32[16,8,128]{2,1,0:T(8,128)S(1)}, ...), condition=%wide.region_7.8_spmd, body=%wide.region_0.7_spmd.sunk | while | flops 236210176 | bytes 6254304 | solution.py:137
  82.2 31.0 %while.33 = (s32[]{:T(128)}, f32[8,128]{1,0:T(8,128)S(1)}, f32[8,128]{1,0:T(8,128)S(1)}, f32[8,128,128]{2,1,0:T(8,128)S(1)}, s32[2048]{0:T(1024)S(1)}, /*index=5...) while((s32[]{:T(128)}, f32[8,128]{1,0:T(8,128)S(1)}, ...), condition=%wide.region_6.6_spmd, body=%wide.region_1.5_spmd.sunk | while | flops 236210176 | bytes 3082573 | solution.py:135
  83.0 1.3 conditional.2
  85.0 1.3 conditional.2
  87.0 1.3 conditional.2
  89.8 1.3 conditional.2
  117.3 31.0 %while.33 = (s32[]{:T(128)}, f32[8,128]{1,0:T(8,128)S(1)}, f32[8,128]{1,0:T(8,128)S(1)}, f32[8,128,128]{2,1,0:T(8,128)S(1)}, s32[2048]{0:T(1024)S(1)}, /*index=5...) while((s32[]{:T(128)}, f32[8,128]{1,0:T(8,128)S(1)}, ...), condition=%wide.region_6.6_spmd, body=%wide.region_1.5_spmd.sunk | while | flops 236210176 | bytes 3082573 | solution.py:135
  118.0 1.3 conditional.2
  120.0 1.3 conditional.2
  122.1 1.3 conditional.2
  126.9 1.3 conditional.2
  130.9 1.3 conditional.2
  132.9 1.3 conditional.2
  134.9 1.3 conditional.2
  136.9 1.3 conditional.2
  139.0 1.3 conditional.2
  141.0 1.3 conditional.2
  145.0 1.3 conditional.2
  152.4 29.8 %while.33 = (s32[]{:T(128)}, f32[8,128]{1,0:T(8,128)S(1)}, f32[8,128]{1,0:T(8,128)S(1)}, f32[8,128,128]{2,1,0:T(8,128)S(1)}, s32[2048]{0:T(1024)S(1)}, /*index=5...) while((s32[]{:T(128)}, f32[8,128]{1,0:T(8,128)S(1)}, ...), condition=%wide.region_6.6_spmd, body=%wide.region_1.5_spmd.sunk | while | flops 236210176 | bytes 3082573 | solution.py:135
  186.2 23.6 %while.33 = (s32[]{:T(128)}, f32[8,128]{1,0:T(8,128)S(1)}, f32[8,128]{1,0:T(8,128)S(1)}, f32[8,128,128]{2,1,0:T(8,128)S(1)}, s32[2048]{0:T(1024)S(1)}, /*index=5...) while((s32[]{:T(128)}, f32[8,128]{1,0:T(8,128)S(1)}, ...), condition=%wide.region_6.6_spmd, body=%wide.region_1.5_spmd.sunk | while | flops 236210176 | bytes 3082573 | solution.py:135
  202.5 1.3 conditional.2
  213.8 28.5 %while.33 = (s32[]{:T(128)}, f32[8,128]{1,0:T(8,128)S(1)}, f32[8,128]{1,0:T(8,128)S(1)}, f32[8,128,128]{2,1,0:T(8,128)S(1)}, s32[2048]{0:T(1024)S(1)}, /*index=5...) while((s32[]{:T(128)}, f32[8,128]{1,0:T(8,128)S(1)}, ...), condition=%wide.region_6.6_spmd, body=%wide.region_1.5_spmd.sunk | while | flops 236210176 | bytes 3082573 | solution.py:135
  215.4 1.3 conditional.2
  220.2 1.3 conditional.2
  246.4 23.5 %while.33 = (s32[]{:T(128)}, f32[8,128]{1,0:T(8,128)S(1)}, f32[8,128]{1,0:T(8,128)S(1)}, f32[8,128,128]{2,1,0:T(8,128)S(1)}, s32[2048]{0:T(1024)S(1)}, /*index=5...) while((s32[]{:T(128)}, f32[8,128]{1,0:T(8,128)S(1)}, ...), condition=%wide.region_6.6_spmd, body=%wide.region_1.5_spmd.sunk | while | flops 236210176 | bytes 3082573 | solution.py:135
  259.1 1.3 conditional.2
  262.6 1.3 conditional.2
  274.0 24.8 %while.33 = (s32[]{:T(128)}, f32[8,128]{1,0:T(8,128)S(1)}, f32[8,128]{1,0:T(8,128)S(1)}, f32[8,128,128]{2,1,0:T(8,128)S(1)}, s32[2048]{0:T(1024)S(1)}, /*index=5...) while((s32[]{:T(128)}, f32[8,128]{1,0:T(8,128)S(1)}, ...), condition=%wide.region_6.6_spmd, body=%wide.region_1.5_spmd.sunk | while | flops 236210176 | bytes 3082573 | solution.py:135
  279.1 1.3 conditional.2
  291.5 1.3 conditional.2
  302.9 23.6 %while.33 = (s32[]{:T(128)}, f32[8,128]{1,0:T(8,128)S(1)}, f32[8,128]{1,0:T(8,128)S(1)}, f32[8,128,128]{2,1,0:T(8,128)S(1)}, s32[2048]{0:T(1024)S(1)}, /*index=5...) while((s32[]{:T(128)}, f32[8,128]{1,0:T(8,128)S(1)}, ...), condition=%wide.region_6.6_spmd, body=%wide.region_1.5_spmd.sunk | while | flops 236210176 | bytes 3082573 | solution.py:135
  315.5 1.3 conditional.2
  319.1 1.3 conditional.2
  330.5 28.5 %while.33 = (s32[]{:T(128)}, f32[8,128]{1,0:T(8,128)S(1)}, f32[8,128]{1,0:T(8,128)S(1)}, f32[8,128,128]{2,1,0:T(8,128)S(1)}, s32[2048]{0:T(1024)S(1)}, /*index=5...) while((s32[]{:T(128)}, f32[8,128]{1,0:T(8,128)S(1)}, ...), condition=%wide.region_6.6_spmd, body=%wide.region_1.5_spmd.sunk | while | flops 236210176 | bytes 3082573 | solution.py:135
  332.0 1.3 conditional.2
  336.8 1.3 conditional.2
  363.0 23.5 %while.33 = (s32[]{:T(128)}, f32[8,128]{1,0:T(8,128)S(1)}, f32[8,128]{1,0:T(8,128)S(1)}, f32[8,128,128]{2,1,0:T(8,128)S(1)}, s32[2048]{0:T(1024)S(1)}, /*index=5...) while((s32[]{:T(128)}, f32[8,128]{1,0:T(8,128)S(1)}, ...), condition=%wide.region_6.6_spmd, body=%wide.region_1.5_spmd.sunk | while | flops 236210176 | bytes 3082573 | solution.py:135
  366.9 1.3 conditional.2
  379.3 1.3 conditional.2
  390.7 29.8 %while.33 = (s32[]{:T(128)}, f32[8,128]{1,0:T(8,128)S(1)}, f32[8,128]{1,0:T(8,128)S(1)}, f32[8,128,128]{2,1,0:T(8,128)S(1)}, s32[2048]{0:T(1024)S(1)}, /*index=5...) while((s32[]{:T(128)}, f32[8,128]{1,0:T(8,128)S(1)}, ...), condition=%wide.region_6.6_spmd, body=%wide.region_1.5_spmd.sunk | while | flops 236210176 | bytes 3082573 | solution.py:135
  391.4 1.3 conditional.2
  419.2 1.3 conditional.2
  424.5 22.3 %while.33 = (s32[]{:T(128)}, f32[8,128]{1,0:T(8,128)S(1)}, f32[8,128]{1,0:T(8,128)S(1)}, f32[8,128,128]{2,1,0:T(8,128)S(1)}, s32[2048]{0:T(1024)S(1)}, /*index=5...) while((s32[]{:T(128)}, f32[8,128]{1,0:T(8,128)S(1)}, ...), condition=%wide.region_6.6_spmd, body=%wide.region_1.5_spmd.sunk | while | flops 236210176 | bytes 3082573 | solution.py:135
  431.1 1.3 conditional.2
  435.9 1.3 conditional.2
  439.5 1.3 conditional.2
  450.9 29.8 %while.33 = (s32[]{:T(128)}, f32[8,128]{1,0:T(8,128)S(1)}, f32[8,128]{1,0:T(8,128)S(1)}, f32[8,128,128]{2,1,0:T(8,128)S(1)}, s32[2048]{0:T(1024)S(1)}, /*index=5...) while((s32[]{:T(128)}, f32[8,128]{1,0:T(8,128)S(1)}, ...), condition=%wide.region_6.6_spmd, body=%wide.region_1.5_spmd.sunk | while | flops 236210176 | bytes 3082573 | solution.py:135
  484.7 29.8 %while.33 = (s32[]{:T(128)}, f32[8,128]{1,0:T(8,128)S(1)}, f32[8,128]{1,0:T(8,128)S(1)}, f32[8,128,128]{2,1,0:T(8,128)S(1)}, s32[2048]{0:T(1024)S(1)}, /*index=5...) while((s32[]{:T(128)}, f32[8,128]{1,0:T(8,128)S(1)}, ...), condition=%wide.region_6.6_spmd, body=%wide.region_1.5_spmd.sunk | while | flops 236210176 | bytes 3082573 | solution.py:135
  485.5 1.3 conditional.2
  487.5 1.3 conditional.2
  509.2 1.3 conditional.2
  518.6 21.1 %while.33 = (s32[]{:T(128)}, f32[8,128]{1,0:T(8,128)S(1)}, f32[8,128]{1,0:T(8,128)S(1)}, f32[8,128,128]{2,1,0:T(8,128)S(1)}, s32[2048]{0:T(1024)S(1)}, /*index=5...) while((s32[]{:T(128)}, f32[8,128]{1,0:T(8,128)S(1)}, ...), condition=%wide.region_6.6_spmd, body=%wide.region_1.5_spmd.sunk | while | flops 236210176 | bytes 3082573 | solution.py:135
  532.3 1.3 conditional.2
  538.4 1.3 conditional.2
  543.7 17.3 %while.33 = (s32[]{:T(128)}, f32[8,128]{1,0:T(8,128)S(1)}, f32[8,128]{1,0:T(8,128)S(1)}, f32[8,128,128]{2,1,0:T(8,128)S(1)}, s32[2048]{0:T(1024)S(1)}, /*index=5...) while((s32[]{:T(128)}, f32[8,128]{1,0:T(8,128)S(1)}, ...), condition=%wide.region_6.6_spmd, body=%wide.region_1.5_spmd.sunk | while | flops 236210176 | bytes 3082573 | solution.py:135
  549.8 1.3 conditional.2
  556.2 1.3 conditional.2
  562.1 3.8 pad_maximum_fusion
  565.9 190.1 %all_to_all.10 = f32[16,8,128,130]{2,1,3,0:T(8,128)S(1)} all-to-all(f32[16,8,128,130]{2,1,3,0:T(8,128)S(1)} %pad_maximum_fusion), channel_id=1, replica_groups=mesh['pb'=16,'ka_0'=2,'ka_1'=8] {'ka_0','ka_1'}, dimensions={0} | all-to-all | bytes 17039360 | tf_op jit(solution)/shard_map/all_to_all | solution.py:61
  (1889 shorter events, 463.9 us)
Async XLA Ops:
  6.5 68.0 %all-gather.3.cloned.1.call-start = ((), (), s32[]{:S(2)}) async-start(), calls=%async_computation.2 | async-start | bytes 4718592 | tf_op jit(solution)/shard_map/all_gather | solution.py:26
  18.2 22.1 %all-to-all-start = ((bf16[16,128,256]{2,1,0:T(8,128)(2,1)}), bf16[16,128,256]{2,1,0:T(8,128)(2,1)S(1)}, u32[]{:S(2)}, u32[]{:S(2)}) async-start(bf16[16,128,256]{2,1,0:T(8,128)(2,1)} %broadcast_in_dim.58), calls=%async_computation | async-start | bytes 2097152 | tf_op jit(solution)/shard_map/all_to_all | solution.py:39
Sparse Core Ops, SparseCore 0:
  16.3 58.1 all-gather.2
where the time goes:
time: 769 us; the launch traced here: 765 us
  blocking collectives  200 us (26%)
  loops' own time  198 us (26%)
  matrix products  175 us (23%)
  local copies, waits for them, and re-layouts  83.2 us (11%)
  waiting for transfers between devices  46.6 us (6%)
  other arithmetic  41.3 us (5%)
  between operations  13.5 us (2%)
  starting transfers between devices  8.12 us (1%)
    all_to_all x1, blocking collectives, side_by_side(): lax.all_to_all(both, axis, split_axis=split_dim, concat_axis=concat_dim,...  190 us
    another operation x16, loops' own time, query_run(): return lax.fori_loop(0, size_query, key_run, empty_state(heads, own_count))  174 us
    dot_general x177, matrix products, tile_update(): jnp.einsum('hqk,kd->hqd', weight, value_rows.astype(jnp.float32), precisi...  132 us
    dot_general x177, matrix products, tile_update(): jnp.einsum('qhd,kd->hqk', grouped, key_rows, preferred_element_type=jnp.f...  42.7 us
    all_gather x1, waiting for transfers between devices, all_blocks(): blocks = lax.all_gather(blocks, axes[k], axis=0, tiled=True)  34.2 us
    dynamic_slice x256, local copies, waits for them, and re-layouts, key_run(): piece_pos = lax.dynamic_slice_in_dim(key_pos, offset, own_count, 0)  19.8 us
    reduce_sum x177, other arithmetic, tile_update(): totals = totals * factor + jnp.sum(weight, axis=2)  18.6 us
    dynamic_update_slice x48, local copies, waits for them, and re-layouts, local_partials(): return lax.map(query_run, jnp.arange(size_key, dtype=jnp.int32))  17.4 us
  transfers between devices with their start and end apart: 2, of which 2 were waited for; matrix products, arithmetic and copies ran while one was open for 0% of the time, Pallas kernels for 0%

commit v1 on v0

v1 whole, which is shorter than its diff:
```python
import functools

import jax
import jax.numpy as jnp
from jax import lax
from jax.experimental import pallas as pl
from jax.experimental.pallas import tpu as pltpu
from jax.sharding import Mesh
from jax.sharding import PartitionSpec as P

AXES = ("yh", "x", "c", "yl", "z")
NX, NC, NY, NZ = 4, 2, 4, 8
NH = NX * NC
HD = 128
RUN = 128
C = 1.4426950408889634 / HD**0.5
F32, BF16 = jnp.float32, jnp.bfloat16
GROUP, REACH = 4, 4
NT = (((1,), (1,)), ((), ()))
LOW, HIGH = 2.0**-60, 2.0**100
EMPTY = -1e30

def places(ranks):
    n = ranks.shape[0]
    place = jnp.sum((ranks[None, :] < ranks[:, None]).astype(jnp.int32), axis=1)
    hit = place[None, :] == jnp.arange(n, dtype=jnp.int32)[:, None]
    order = jnp.sum(jnp.where(hit, jnp.arange(n, dtype=jnp.int32)[None, :], 0), axis=1)
    held = jnp.sum(jnp.where(hit, ranks[None, :], 0), axis=1)
    return order, held

def plan(q_ranks, k_ranks, group, reach):
    q_order, q_held = places(q_ranks)
    k_order, k_held = places(k_ranks)
    seen = jnp.sum((k_ranks[None, :] <= q_held[:, None]).astype(jnp.int32), axis=1)
    tops = seen[group - 1 :: group]
    chunks = jnp.maximum((tops + reach - 1) // reach, 1)
    pad = jnp.zeros((group,), jnp.int32)
    return jnp.concatenate([
        q_order, pad, q_held, pad - 1, k_order, k_held, seen, pad, chunks, jnp.ones((1,), jnp.int32),
        jnp.sum(chunks)[None],
    ])

def attend(group, reach, n_q, n_k, meta, q_ref, k_ref, v_ref, out_ref, s0, s1, acc, sums):
    blocks = n_q // group
    o_q, o_qr = 0, n_q + group
    o_k = 2 * (n_q + group)
    o_kr = o_k + n_k
    o_seen = o_kr + n_k
    o_ch = o_seen + n_q + group
    o_tot = o_ch + blocks + 1
    diff = lax.broadcasted_iota(jnp.int32, (RUN, RUN), 1) - lax.broadcasted_iota(jnp.int32, (RUN, RUN), 0)

    def rows_q(b):
        return jnp.concatenate([q_ref[meta[o_q + b * group + g]] for g in range(group)], axis=0)

    def rows_k(ref, j):
        return jnp.concatenate([ref[meta[o_k + j * reach + r]] for r in range(reach)], axis=0)

    def scores(b, j, s_ref):
        s_ref[...] = lax.dot_general(rows_q(b), rows_k(k_ref, j), NT, preferred_element_type=F32)

    def weigh(b, j, s_ref):
        high, low, part = [], [], []
        for g in range(group):
            own = meta[o_qr + b * group + g]
            row_h, row_l, row_s = [], [], None
            for r in range(reach):
                gap = (own - meta[o_kr + j * reach + r]) * RUN
                s = s_ref[g * RUN : (g + 1) * RUN, r * RUN : (r + 1) * RUN]
                p = jnp.where(diff <= gap, jnp.exp2(s * C), 0.0)
                h = p.astype(BF16)
                row_h.append(h)
                row_l.append((p - h.astype(F32)).astype(BF16))
                row_s = p if row_s is None else row_s + p
            high.append(jnp.concatenate(row_h, axis=1))
            low.append(jnp.concatenate(row_l, axis=1))
            part.append(row_s)
        v = rows_k(v_ref, j)
        new = jnp.dot(jnp.concatenate(high, axis=0), v, preferred_element_type=F32)
        new += jnp.dot(jnp.concatenate(low, axis=0), v, preferred_element_type=F32)
        at = pl.ds(pl.multiple_of(b * group * RUN, RUN), group * RUN)
        first = j == 0
        acc[at, :] = jnp.where(first, 0.0, acc[at, :]) + new
        sums[at, :] = jnp.where(first, 0.0, sums[at, :]) + jnp.concatenate(part, axis=0)

    def after(b, j):
        b = jnp.minimum(b, blocks)
        last = j + 1 >= meta[o_ch + b]
        return jnp.minimum(jnp.where(last, b + 1, b), blocks), jnp.where(last, 0, j + 1)

    scores(0, 0, s0)

    def pair(_, at):
        b, j = at
        b1, j1 = after(b, j)
        scores(b1, j1, s1)
        weigh(b, j, s0)
        b2, j2 = after(b1, j1)
        scores(b2, j2, s0)
        weigh(b1, j1, s1)
        return b2, j2

    lax.fori_loop(0, (meta[o_tot] + 1) // 2, pair, (jnp.int32(0), jnp.int32(0)))

    def close(p, _):
        at = pl.ds(pl.multiple_of(p * RUN, RUN), RUN)
        slot = meta[o_q + p]
        seen = meta[o_seen + p]
        total = jnp.sum(sums[at, :].T, axis=0, keepdims=True)
        out_ref[slot, :RUN, :] = acc[at, :]
        peak = jnp.where(seen > 0, 0.0, EMPTY)
        out_ref[slot, RUN:, :] = jnp.concatenate([total, jnp.full((7, RUN), peak, F32)], axis=0)
        good = jnp.logical_and(total > LOW, total < HIGH)
        bad = jnp.sum(jnp.where(good, 0.0, 1.0)) > 0.0

        @pl.when(jnp.logical_and(bad, seen > 0))
        def _():
            q = q_ref[slot]
            own = meta[o_qr + p]

            def step(i, state):
                top, tot, got = state
                run = meta[o_k + i]
                gap = (own - meta[o_kr + i]) * RUN
                s = lax.dot_general(q, k_ref[run], NT, preferred_element_type=F32) * C
                keep = diff <= gap
                s = jnp.where(keep, s, EMPTY)
                new = jnp.maximum(top, jnp.max(s, axis=1, keepdims=True))
                w = jnp.where(keep, jnp.exp2(s - new), 0.0)
                f = jnp.exp2(top - new)
                h = w.astype(BF16)
                l = (w - h.astype(F32)).astype(BF16)
                v = v_ref[run]
                got = got * f + (jnp.dot(h, v, preferred_element_type=F32) + jnp.dot(l, v, preferred_element_type=F32))
                return new, tot * f + jnp.sum(w, axis=1, keepdims=True), got

            zero = jnp.zeros((RUN, 1), F32)
            top, tot, got = lax.fori_loop(0, seen, step, (zero + EMPTY, zero, jnp.zeros((RUN, HD), F32)))
            out_ref[slot, :RUN, :] = got
            wide = jnp.broadcast_to(tot, (RUN, RUN)).T
            peaks = jnp.broadcast_to(top, (RUN, RUN)).T
            out_ref[slot, RUN:, :] = jnp.concatenate([wide[:1], peaks[:7]], axis=0)

        return 0

    lax.fori_loop(0, n_q, close, 0)

def attend_call(meta, q, k, v, group, reach):
    n_q, n_k = q.shape[0], k.shape[0]
    vm = pl.BlockSpec(memory_space=pltpu.VMEM)
    return pl.pallas_call(
        functools.partial(attend, group, reach, n_q, n_k),
        out_shape=jax.ShapeDtypeStruct((n_q, RUN + 8, HD), F32),
        in_specs=[pl.BlockSpec(memory_space=pltpu.SMEM), vm, vm, vm],
        out_specs=vm,
        scratch_shapes=[
            pltpu.VMEM((group * RUN, reach * RUN), F32),
            pltpu.VMEM((group * RUN, reach * RUN), F32),
            pltpu.VMEM(((n_q + group) * RUN, HD), F32),
            pltpu.VMEM(((n_q + group) * RUN, RUN), F32),
        ],
        compiler_params=pltpu.CompilerParams(vmem_limit_bytes=50 << 20),
        name="attend",
    )(meta, q, k, v)


def here():
    y = lax.axis_index("yh") * 2 + lax.axis_index("yl")
    return lax.axis_index("x"), lax.axis_index("c"), y, lax.axis_index("z")


def device(x, c, y, z):
    return {"yh": y // 2, "x": x, "c": c, "yl": y % 2, "z": z}


def remote(src, dst, send_sem, recv_sem, target):
    return pltpu.make_async_remote_copy(
        src_ref=src, dst_ref=dst, send_sem=send_sem, recv_sem=recv_sem,
        device_id=device(*target), device_id_type=pl.DeviceIdType.MESH,
    )


def near_first(t, n):
    odd = t % 2
    return odd * ((t + 1) // 2) + (1 - odd) * ((n - t // 2) % n)


def spread(q_ref, k_ref, v_ref, qo, ko, vo, q_in, k_in, l_in, u_in, c_in, q_s1, q_s2, k_s1, k_s2, l_s1, l_s2, u_s1, u_s2, c_out):
    x, c, y, z = here()
    lane = x * NC + c
    half = RUN // 2
    low, up = pl.ds(0, half), pl.ds(half, half)

    barrier = pltpu.get_barrier_semaphore()
    for d in range(1, NZ):
        pl.semaphore_signal(barrier, 1, device_id=device(x, c, y, (z + d) % NZ), device_id_type=pl.DeviceIdType.MESH)
    for d in range(1, NH):
        to = (lane + d) % NH
        pl.semaphore_signal(barrier, 1, device_id=device(to // NC, to % NC, y, z), device_id_type=pl.DeviceIdType.MESH)
    for d in range(1, NY):
        pl.semaphore_signal(barrier, 1, device_id=device(x, c, (y + d) % NY, z), device_id_type=pl.DeviceIdType.MESH)
    pl.semaphore_wait(barrier, NZ + NH + NY - 3)

    def slot(xx, zz):
        return (xx * NC + c) * NZ + zz

    def q_cols(h):
        return q_ref.at[:, pl.ds(pl.multiple_of(h * HD, HD), HD)]

    own_q = qo.at[y * NH + lane]
    mine = slot(x, z)

    def k_first(d):
        return remote(k_ref, ko.at[mine], k_s1.at[d], k_in.at[x, z], (x, c, y, (z + d) % NZ))

    def l_first(d):
        return remote(v_ref.at[low, :], vo.at[mine, low, :], l_s1.at[d], l_in.at[x, z], (x, c, y, (z + d) % NZ))

    def u_first(d):
        return remote(v_ref.at[up, :], vo.at[mine, up, :], u_s1.at[d], u_in.at[x, z], ((x + d) % NX, c, y, z))

    def q_first(d):
        to = (lane + d) % NH
        return remote(q_cols(to), own_q, q_s1.at[d], q_in.at[y, lane], (to // NC, to % NC, y, z))

    for d in (1, 3, 2):
        u_first(d).start()
    for d in range(1, NH):
        q_first(d).start()
    for d in (1, 7, 2, 6, 3, 5, 4):
        k_first(d).start()
        l_first(d).start()
    pltpu.make_async_copy(k_ref, ko.at[mine], k_in.at[x, z]).start()
    pltpu.make_async_copy(v_ref.at[low, :], vo.at[mine, low, :], l_in.at[x, z]).start()
    pltpu.make_async_copy(v_ref.at[up, :], vo.at[mine, up, :], u_in.at[x, z]).start()
    pltpu.make_async_copy(q_cols(lane), own_q, q_in.at[y, lane]).start()

    def k_next(zz, d):
        s = slot(x, zz)
        return remote(ko.at[s], ko.at[s], k_s2.at[d, zz], k_in.at[x, zz], ((x + d) % NX, c, y, z))

    def l_next(zz, d):
        s = slot(x, zz)
        return remote(vo.at[s, low, :], vo.at[s, low, :], l_s2.at[d, zz], l_in.at[x, zz], ((x + d) % NX, c, y, z))

    def u_next(xx, d):
        s = slot(xx, z)
        return remote(vo.at[s, up, :], vo.at[s, up, :], u_s2.at[d, xx], u_in.at[xx, z], (x, c, y, (z + d) % NZ))

    def q_next(h, d):
        s = y * NH + h
        return remote(qo.at[s], qo.at[s], q_s2.at[d, h], q_in.at[y, h], (x, c, (y + d) % NY, z))

    def got_k(xx, zz):
        s = slot(xx, zz)
        pltpu.make_async_copy(ko.at[s], ko.at[s], k_in.at[xx, zz]).wait()
        pltpu.make_async_copy(vo.at[s, low, :], vo.at[s, low, :], l_in.at[xx, zz]).wait()

    def got_u(xx, zz):
        s = slot(xx, zz)
        pltpu.make_async_copy(vo.at[s, up, :], vo.at[s, up, :], u_in.at[xx, zz]).wait()

    def got_q(yy, h):
        s = yy * NH + h
        pltpu.make_async_copy(qo.at[s], qo.at[s], q_in.at[yy, h]).wait()

    def relay(t, _):
        zz = (z + near_first(t, NZ)) % NZ
        got_k(x, zz)
        for d in (1, 3, 2):
            k_next(zz, d).start()
            l_next(zz, d).start()
        h = (lane + near_first(t, NH)) % NH
        got_q(y, h)
        for d in (1, 3, 2):
            q_next(h, d).start()
        return 0

    def relay_up(t, _):
        xx = (x + near_first(t, NX)) % NX
        got_u(xx, z)
        for d in (1, 7, 2, 6, 3, 5, 4):
            u_next(xx, d).start()
        return 0

    lax.fori_loop(0, 3, relay, 0)
    lax.fori_loop(0, NX, relay_up, 0)
    lax.fori_loop(3, NZ, relay, 0)

    def share(xx, half_of, ref):
        part = pl.ds(pl.multiple_of(slot(xx, 0), NZ), NZ)
        return remote(ref.at[part], ref.at[part], c_out.at[half_of, xx], c_in.at[half_of, xx], (x, 1 - c, y, z))

    def pass_on(t, _):
        xx = (x + near_first(t, NX)) % NX

        @pl.when(t > 0)
        def _():
            lax.fori_loop(0, NZ, lambda i, _: (got_k(xx, i), 0)[1], 0)

        lax.fori_loop(1, NZ, lambda i, _: (got_u(xx, (z + i) % NZ), 0)[1], 0)
        share(xx, 0, ko).start()
        share(xx, 1, vo).start()
        return 0

    lax.fori_loop(0, NX, pass_on, 0)

    def all_q(t, _):
        lax.fori_loop(0, NH, lambda h, _: (got_q((y + t) % NY, h), 0)[1], 0)
        return 0

    lax.fori_loop(1, NY, all_q, 0)

    def shared(xx, _):
        share(xx, 0, ko).wait_send()
        share(xx, 1, vo).wait_send()
        other = pl.ds(pl.multiple_of((xx * NC + 1 - c) * NZ, NZ), NZ)
        pltpu.make_async_copy(ko.at[other], ko.at[other], c_in.at[0, xx]).wait()
        pltpu.make_async_copy(vo.at[other], vo.at[other], c_in.at[1, xx]).wait()
        return 0

    lax.fori_loop(0, NX, shared, 0)

    for d in range(1, NX):
        u_first(d).wait_send()
    for d in range(1, NH):
        q_first(d).wait_send()
    for d in range(1, NZ):
        k_first(d).wait_send()
        l_first(d).wait_send()

    def sent(i, _):
        for d in range(1, NX):
            k_next(i, d).wait_send()
            l_next(i, d).wait_send()
            q_next(i, d).wait_send()
        return 0

    lax.fori_loop(0, NZ, sent, 0)

    def sent_up(i, _):
        for d in range(1, NZ):
            u_next(i, d).wait_send()
        return 0

    lax.fori_loop(0, NX, sent_up, 0)


def spread_call(q, k, v):
    vm = pl.BlockSpec(memory_space=pltpu.VMEM)
    anywhere = pl.BlockSpec(memory_space=pl.ANY)
    dma = pltpu.SemaphoreType.DMA
    return pl.pallas_call(
        spread,
        out_shape=(
            jax.ShapeDtypeStruct((NY * NH, RUN, HD), BF16),
            jax.ShapeDtypeStruct((NH * NZ, RUN, HD), BF16),
            jax.ShapeDtypeStruct((NH * NZ, RUN, HD), BF16),
        ),
        in_specs=[anywhere] * 3,
        out_specs=(vm, vm, vm),
        scratch_shapes=[
            dma((NY, NH)), dma((NX, NZ)), dma((NX, NZ)), dma((NX, NZ)), dma((2, NX)),
            dma((NH,)), dma((NY, NH)), dma((NZ,)), dma((NX, NZ)), dma((NZ,)), dma((NX, NZ)),
            dma((NX,)), dma((NZ, NX)), dma((2, NX)),
        ],
        compiler_params=pltpu.CompilerParams(collective_id=1, has_side_effects=True, vmem_limit_bytes=24 << 20),
        name="spread",
    )(q, k, v)


def gather_parts(p_ref, o_ref, got, send_sem, recv_sem):
    x, c, y, z = here()
    n = NY * NH
    me = y * NH + x * NC + c

    def target(t):
        to = (me + t) % n
        return to, (to // NC % NX, to % NC, to // NH, z)

    barrier = pltpu.get_barrier_semaphore()

    def greet(t, _):
        pl.semaphore_signal(barrier, 1, device_id=device(*target(t)[1]), device_id_type=pl.DeviceIdType.MESH)
        return 0

    lax.fori_loop(1, n, greet, 0)
    pl.semaphore_wait(barrier, n - 1)

    def part(t):
        to, where = target(t)
        return remote(p_ref.at[to], got.at[me], send_sem.at[t], recv_sem.at[me], where)

    lax.fori_loop(1, n, lambda t, _: (part(t).start(), 0)[1], 0)
    pltpu.make_async_copy(p_ref.at[me], got.at[me], recv_sem.at[me]).start()
    lax.fori_loop(0, n, lambda i, _: (pltpu.make_async_copy(got.at[i], got.at[i], recv_sem.at[i]).wait(), 0)[1], 0)

    rows = []
    for h in range(NH):
        totals = [got[s * NH + h, RUN : RUN + 1, :] for s in range(NY)]
        tops = [got[s * NH + h, RUN + 1 : RUN + 2, :] for s in range(NY)]
        top = functools.reduce(jnp.maximum, tops)
        factors = [jnp.exp2(t - top) for t in tops]
        whole = functools.reduce(jnp.add, [f * t for f, t in zip(factors, totals)])
        rows += [f / whole for f in factors]
    weights = jnp.concatenate(rows + [jnp.zeros((RUN - n, RUN), F32)], axis=0).T
    for h in range(NH):
        o_ref[:, h * HD : (h + 1) * HD] = functools.reduce(
            jnp.add, [got[s * NH + h, :RUN, :] * weights[:, h * NY + s : h * NY + s + 1] for s in range(NY)]
        )

    lax.fori_loop(1, n, lambda t, _: (part(t).wait_send(), 0)[1], 0)


def gather_call(parts):
    n = NY * NH
    return pl.pallas_call(
        gather_parts,
        out_shape=jax.ShapeDtypeStruct((RUN, NH * HD), F32),
        in_specs=[pl.BlockSpec(memory_space=pl.ANY)],
        out_specs=pl.BlockSpec(memory_space=pltpu.VMEM),
        scratch_shapes=[
            pltpu.VMEM((n, RUN + 8, HD), F32), pltpu.SemaphoreType.DMA((n,)), pltpu.SemaphoreType.DMA((n,)),
        ],
        compiler_params=pltpu.CompilerParams(collective_id=2, has_side_effects=True, vmem_limit_bytes=16 << 20),
        name="gather_parts",
    )(parts)


def on_device(queries, keys, values, positions):
    ranks = (positions.reshape(-1, RUN)[:, 0] // RUN).reshape(2, NX, NC, 2, NZ)
    yh, yl, z = lax.axis_index("yh"), lax.axis_index("yl"), lax.axis_index("z")
    q_ranks = lax.dynamic_index_in_dim(ranks, z, 4, False).transpose(0, 3, 1, 2).reshape(-1)
    k_ranks = lax.dynamic_index_in_dim(lax.dynamic_index_in_dim(ranks, yh, 0, False), yl, 2, False).reshape(-1)
    meta = plan(q_ranks, k_ranks, GROUP, REACH)
    q, k, v = spread_call(queries, keys, values)
    return gather_call(attend_call(meta, q, k, v, GROUP, REACH))


def solution(mesh):
    finer = Mesh(mesh.devices.reshape(2, NX, NC, 2, NZ), AXES)
    placed = (P(AXES, None), P(AXES, None), P(AXES, None), P())
    return jax.shard_map(on_device, mesh=finer, in_specs=placed, out_specs=P(AXES, None), check_vma=False)
```

time: 769 us -> 614 us (0.80)
  the two profiles are of different devices: /device:TPU:19 before, /device:TPU:161 now
where the time goes in v1:
time: 614 us
  Pallas kernels  604 us (98%)
  local copies, waits for them, and re-layouts  8.66 us (1%)
    pallas_call x1, Pallas kernels, attend_call(): pl.pallas_call(functools.partial(attend, group, reach, n_q, n_k), out_sha...  494 us
    pallas_call x1, Pallas kernels, gather_call(): pl.pallas_call(gather_parts, out_shape=jax.ShapeDtypeStruct((RUN, NH * HD...  77.4 us
    pallas_call x1, Pallas kernels, spread_call(): pl.pallas_call(spread, out_shape=(jax.ShapeDtypeStruct((NY * NH, RUN, HD)...  32.3 us

profile of v1, /device:TPU:161, one launch (start us, length us, event | category | flops | bytes accessed | tf_op | source)
XLA Modules:
  0.0 613.8 jit_solution(9227492543244829144)
XLA Ops:
  0.0 1.0 slice_reduce_fusion
  1.0 0.1 squeeze.11
  1.2 0.1 lt.49
  1.3 0.1 constant_dynamic-slice_fusion
  1.4 0.1 copy.11
  1.5 0.2 convert_reduce_fusion
  1.7 0.1 select_reduce_fusion
  1.8 0.1 copy.12
  1.9 0.1 lt.43
  2.0 0.2 convert_reduce_fusion.2
  2.2 0.1 select_reduce_fusion.2
  2.3 0.2 convert_reduce_fusion.1
  2.5 0.1 slice.7
  2.6 0.7 fusion.1
  3.3 0.7 concatenate.3.meta
  4.0 0.0 copy-start.2
  4.0 0.9 copy-done.2
  5.0 0.0 copy-start.3
  5.0 0.8 copy-done.3
  5.7 0.0 copy-start.4
  5.7 0.8 copy-done.4
  6.5 32.3 %spread.1 = (bf16[32,128,128]{2,1,0:T(8,128)(2,1)S(1)}, bf16[64,128,128]{2,1,0:T(8,128)(2,1)S(1)}, bf16[64,128,128]{2,1,0:T(8,128)(2,1)S(1)}) custom-call(bf16[128,1024]{1,0:T(8,128)(2,1)S(1)} %copy-done.2, bf16[128,128]{1,0:T(8,128)(2,1)S(1)} %copy-done.3, bf16[128,128]{1,0:T(8,128)(2,1)S(1)} %copy-done.4), custom_call_target="tpu_custom_call" | custom-call | tf_op jit(solution)/shard_map/spread/pallas_call | solution.py:353
  38.8 0.0 copy-start.1
  38.8 1.3 copy-done.1
  40.1 493.8 %attend.1.p_ref = f32[32,136,128]{2,1,0:T(8,128)} custom-call(s32[246]{0:T(256)S(1)} %concatenate.3.meta, bf16[32,128,128]{2,1,0:T(8,128)(2,1)S(1)} %get-tuple-element.8.q_ref, bf16[64,128,128]{2,1,0:T(8,128)(2,1)S(1)} %get-tuple-element.9.k_ref, bf16[64,128,128]{2,1,0:T(8,128)(2,1)} %copy-done.1), custom_call_target="tpu_custom_call" | custom-call | tf_op jit(solution)/shard_map/attend/pallas_call | solution.py:151
  534.0 0.0 copy-start
  534.0 1.6 copy-done
  535.6 77.4 %gather_parts.1 = f32[128,1024]{1,0:T(8,128)S(1)} custom-call(f32[32,136,128]{2,1,0:T(8,128)S(1)} %copy-done), custom_call_target="tpu_custom_call" | custom-call | tf_op jit(solution)/shard_map/gather_parts/pallas_call | solution.py:417
  613.0 0.8 copy.14
  (4 shorter events, 0.1 us)
Async XLA Ops:
  4.0 1.0 copy-start.2
  5.0 0.8 copy-start.3
  5.7 0.8 copy-start.4
  38.8 1.3 copy-start.1
  534.0 1.6 copy-start

commit v2 on v1

v2 whole, which is shorter than its diff:
```python
import functools

import jax
import jax.numpy as jnp
from jax import lax
from jax.experimental import pallas as pl
from jax.experimental.pallas import tpu as pltpu
from jax.sharding import Mesh
from jax.sharding import PartitionSpec as P

AXES = ("yh", "x", "c", "yl", "z")
NX, NC, NY, NZ = 4, 2, 4, 8
NH = NX * NC
HD = 128
RUN = 128
C = 1.4426950408889634 / HD**0.5
F32, BF16 = jnp.float32, jnp.bfloat16
GROUP, REACH = 4, 8
NT = (((1,), (1,)), ((), ()))
LOW, HIGH = 2.0**-60, 2.0**100
EMPTY = -1e30
STEPS, TINY = 32767.0, 2.0**-110

def plan(pos_ref, meta, n_q):
    x, c, y, z = here()
    n = pos_ref.shape[0]
    first = pos_ref[...].astype(F32) * (1.0 / RUN)
    column = first[:, :1]
    row = jnp.concatenate([first[i : i + RUN].T[:1] for i in range(0, n, RUN)], axis=1)

    def coords(axis, shape):
        i = lax.broadcasted_iota(jnp.int32, shape, axis)
        iz, iyl, ic, ix, iyh = i % NZ, i // NZ % 2, i // (2 * NZ) % NC, i // (2 * NZ * NC) % NX, i // (2 * NZ * NC * NX)
        iy = 2 * iyh + iyl
        return iz == z, iy == y, iy * NH + ix * NC + ic, (ix * NC + ic) * NZ + iz

    q_row, k_row, _, _ = coords(1, (1, n))
    q_col, k_col, q_slot, k_slot = coords(0, (n, 1))
    below = row < column

    def count(mask):
        return jnp.sum(jnp.where(mask, 1.0, 0.0), axis=1, keepdims=True)

    spot = lax.broadcasted_iota(jnp.int32, (1, RUN), 1).astype(F32)

    def sorted_by_rank(here_col, here_row, things):
        place = count(jnp.logical_and(below, here_row))
        hit = jnp.logical_and(place == spot, here_col)
        return [jnp.sum(jnp.where(hit, thing, 0.0), axis=0, keepdims=True) for thing in things]

    seen = count(jnp.logical_and(row <= column, k_row))
    order, held, sees = sorted_by_rank(q_col, q_row, (q_slot.astype(F32), column, seen))
    held = jnp.where(spot < n_q, held, -1.0)
    rows = [order, held, sees] + sorted_by_rank(k_col, k_row, (k_slot.astype(F32), column))
    meta[...] = jnp.concatenate(rows + [jnp.zeros((3, RUN), F32)], axis=0).astype(jnp.int32)


def attend(group, reach, n_q, n_k, pos_ref, q_ref, k_ref, v_ref, out_ref, stat_ref, s0, s1, acc, sums, found, meta, sem):
    blocks = n_q // group
    plan(pos_ref, found, n_q)
    copy = pltpu.make_async_copy(found, meta, sem)
    copy.start()
    copy.wait()

    def chunks(b):
        top = meta[2, jnp.minimum(b * group + group - 1, n_q - 1)]
        return jnp.where(b < blocks, jnp.maximum((top + reach - 1) // reach, 1), 1)

    diff = lax.broadcasted_iota(jnp.int32, (RUN, RUN), 1) - lax.broadcasted_iota(jnp.int32, (RUN, RUN), 0)

    def rows_q(b):
        return jnp.concatenate([q_ref[meta[0, b * group + g]] for g in range(group)], axis=0)

    def rows_k(ref, j):
        return jnp.concatenate([ref[meta[3, j * reach + r]] for r in range(reach)], axis=0)

    def scores(b, j, s_ref):
        s_ref[...] = lax.dot_general(rows_q(b), rows_k(k_ref, j), NT, preferred_element_type=F32)

    def weigh(b, j, s_ref):
        both, part = [], []
        for g in range(group):
            own = meta[1, b * group + g]
            row_h, row_l, row_s = [], [], None
            for r in range(reach):
                gap = (own - meta[4, j * reach + r]) * RUN
                s = s_ref[g * RUN : (g + 1) * RUN, r * RUN : (r + 1) * RUN]
                p = jnp.where(diff <= gap, jnp.exp2(s * C), 0.0)
                h = p.astype(BF16)
                row_h.append(h)
                row_l.append((p - h.astype(F32)).astype(BF16))
                row_s = p if row_s is None else row_s + p
            both.append(jnp.concatenate([x for pair in zip(row_h, row_l) for x in pair], axis=1))
            part.append(row_s)
        twice = jnp.concatenate([v_ref[meta[3, j * reach + r]] for r in range(reach) for _ in range(2)], axis=0)
        new = jnp.dot(jnp.concatenate(both, axis=0), twice, preferred_element_type=F32)
        at = pl.ds(pl.multiple_of(b * group * RUN, RUN), group * RUN)
        first = j == 0
        acc[at, :] = jnp.where(first, 0.0, acc[at, :]) + new
        sums[at, :] = jnp.where(first, 0.0, sums[at, :]) + jnp.concatenate(part, axis=0)

    def after(b, j):
        b = jnp.minimum(b, blocks)
        last = j + 1 >= chunks(b)
        return jnp.minimum(jnp.where(last, b + 1, b), blocks), jnp.where(last, 0, j + 1)

    total_chunks = functools.reduce(jnp.add, [chunks(b) for b in range(blocks)])
    scores(0, 0, s0)

    def pair(_, at):
        b, j = at
        b1, j1 = after(b, j)
        weigh(b, j, s0)
        scores(b1, j1, s1)
        b2, j2 = after(b1, j1)
        weigh(b1, j1, s1)
        scores(b2, j2, s0)
        return b2, j2

    lax.fori_loop(0, (total_chunks + 1) // 2, pair, (jnp.int32(0), jnp.int32(0)))

    lanes = lax.broadcasted_iota(jnp.int32, (RUN, RUN), 1)

    def coded(got, total):
        mean = got * jnp.where(total > 0.0, 1.0 / total, 0.0)
        reach_of = jnp.maximum(jnp.max(jnp.abs(mean), axis=1, keepdims=True), TINY)
        return jnp.round(mean * (STEPS / reach_of)).astype(jnp.int32).astype(jnp.int16), reach_of

    def close(p, table):
        at = pl.ds(pl.multiple_of(p * RUN, RUN), RUN)
        total = jnp.sum(sums[at, :], axis=1, keepdims=True)
        out_ref[meta[0, p]], widest = coded(acc[at, :], total)
        return jnp.where(lanes == 2 * p, total, jnp.where(lanes == 2 * p + 1, widest, table))

    table = lax.fori_loop(0, n_q, close, jnp.zeros((RUN, RUN), F32), unroll=4).T
    outside = jnp.zeros((1, RUN), F32)
    for p in range(n_q):
        seen = meta[2, p] > 0
        total = table[2 * p : 2 * p + 1]
        good = jnp.logical_and(total > LOW, total < HIGH)
        outside += jnp.where(good, 0.0, jnp.where(seen, 1.0, 0.0))
        peak = jnp.full((6, RUN), jnp.where(seen, 0.0, EMPTY), F32)
        stat_ref[meta[0, p]] = jnp.concatenate([table[2 * p : 2 * p + 2], peak], axis=0)

    @pl.when(jnp.sum(outside) > 0.0)
    def _():
        def again(p, _):
            slot = meta[0, p]
            q = q_ref[slot]
            own = meta[1, p]

            def step(i, state):
                top, tot, got = state
                run = meta[3, i]
                gap = (own - meta[4, i]) * RUN
                s = lax.dot_general(q, k_ref[run], NT, preferred_element_type=F32) * C
                keep = diff <= gap
                s = jnp.where(keep, s, EMPTY)
                new = jnp.maximum(top, jnp.max(s, axis=1, keepdims=True))
                w = jnp.where(keep, jnp.exp2(s - new), 0.0)
                f = jnp.exp2(top - new)
                h = w.astype(BF16)
                l = (w - h.astype(F32)).astype(BF16)
                v = v_ref[run]
                got = got * f + (jnp.dot(h, v, preferred_element_type=F32) + jnp.dot(l, v, preferred_element_type=F32))
                return new, tot * f + jnp.sum(w, axis=1, keepdims=True), got

            zero = jnp.zeros((RUN, 1), F32)
            top, tot, got = lax.fori_loop(0, meta[2, p], step, (zero + EMPTY, zero, jnp.zeros((RUN, HD), F32)))
            out_ref[slot], widest = coded(got, tot)
            stat_ref[slot] = jnp.where(lanes == 0, tot, jnp.where(lanes == 1, widest, top)).T[:8]
            return 0

        lax.fori_loop(0, n_q, again, 0)


def attend_call(first, q, k, v, group, reach):
    n_q, n_k = q.shape[0], k.shape[0]
    vm = pl.BlockSpec(memory_space=pltpu.VMEM)
    return pl.pallas_call(
        functools.partial(attend, group, reach, n_q, n_k),
        out_shape=(
            jax.ShapeDtypeStruct((n_q, RUN, HD), jnp.int16),
            jax.ShapeDtypeStruct((n_q, 8, RUN), F32),
        ),
        in_specs=[vm, vm, vm, vm],
        out_specs=(vm, vm),
        scratch_shapes=[
            pltpu.VMEM((group * RUN, reach * RUN), F32),
            pltpu.VMEM((group * RUN, reach * RUN), F32),
            pltpu.VMEM(((n_q + group) * RUN, HD), F32),
            pltpu.VMEM(((n_q + group) * RUN, RUN), F32),
            pltpu.VMEM((8, RUN), jnp.int32),
            pltpu.SMEM((8, RUN), jnp.int32),
            pltpu.SemaphoreType.DMA,
        ],
        compiler_params=pltpu.CompilerParams(vmem_limit_bytes=20 << 20),
        name="attend",
    )(first, q, k, v)


def here():
    y = lax.axis_index("yh") * 2 + lax.axis_index("yl")
    return lax.axis_index("x"), lax.axis_index("c"), y, lax.axis_index("z")


def device(x, c, y, z):
    return {"yh": y // 2, "x": x, "c": c, "yl": y % 2, "z": z}


def remote(src, dst, send_sem, recv_sem, target):
    return pltpu.make_async_remote_copy(
        src_ref=src, dst_ref=dst, send_sem=send_sem, recv_sem=recv_sem,
        device_id=device(*target), device_id_type=pl.DeviceIdType.MESH,
    )


def spread(q_ref, k_ref, v_ref, qo, ko, vo, q_in, k_in, v_in, kc_in, vc_in, q_near, q_far, k_z, k_x, v_x, v_z, k_c, v_c):
    x, c, y, z = here()
    lane = x * NC + c

    barrier = pltpu.get_barrier_semaphore()

    def greet(*where):
        pl.semaphore_signal(barrier, 1, device_id=device(*where), device_id_type=pl.DeviceIdType.MESH)

    for d in range(1, NZ):
        greet(x, c, y, (z + d) % NZ)
    for d in range(1, NH):
        to = (lane + d) % NH
        greet(to // NC, to % NC, y, z)
    for d in range(1, NY):
        greet(x, c, (y + d) % NY, z)
    pl.semaphore_wait(barrier, NZ + NH + NY - 3)

    def go(copy):
        copy.start()

    def at_x(d):
        return (x + d) % NX

    def at_z(d):
        return (z + d) % NZ

    def slot(dx, dz):
        return (at_x(dx) * NC + c) * NZ + at_z(dz)

    def k_to_x(dz, d):
        s = slot(0, dz)
        go(remote(ko.at[s], ko.at[s], k_x, k_in.at[x, at_z(dz)], (at_x(d), c, y, z)))

    def v_to_z(dx, dz, d):
        s = slot(dx, dz)
        go(remote(vo.at[s], vo.at[s], v_z, v_in.at[at_x(dx), at_z(dz)], (x, c, y, at_z(d))))

    def share(dx, dz, ref, out, into):
        s = slot(dx, dz)
        go(remote(ref.at[s], ref.at[s], out, into, (x, 1 - c, y, z)))

    def got(ref, s, sem):
        pltpu.make_async_copy(ref.at[s], ref.at[s], sem).wait()

    def got_k(dx, dz):
        got(ko, slot(dx, dz), k_in.at[at_x(dx), at_z(dz)])

    def got_v(dx, dz):
        got(vo, slot(dx, dz), v_in.at[at_x(dx), at_z(dz)])

    def got_q(d, h):
        yy = (y + d) % NY
        got(qo, yy * NH + h, q_in.at[yy, h])

    def q_cols(h):
        return q_ref.at[:, pl.ds(pl.multiple_of(h * HD, HD), HD)]

    own_q, own = qo.at[y * NH + lane], slot(0, 0)
    for d in (1, 3, 2):
        go(remote(v_ref, vo.at[own], v_x, v_in.at[x, z], (at_x(d), c, y, z)))
    for d in (1, NZ - 1, 2, NZ - 2, 3, NZ - 3, 4):
        go(remote(k_ref, ko.at[own], k_z, k_in.at[x, z], (x, c, y, at_z(d))))
    for d in range(1, NH):
        to = (lane + d) % NH
        go(remote(q_cols(to), own_q, q_near, q_in.at[y, lane], (to // NC, to % NC, y, z)))
    pltpu.make_async_copy(k_ref, ko.at[own], k_in.at[x, z]).start()
    pltpu.make_async_copy(v_ref, vo.at[own], v_in.at[x, z]).start()
    pltpu.make_async_copy(q_cols(lane), own_q, q_in.at[y, lane]).start()

    def side(t):
        d = (t + 1) // 2
        return d if t % 2 else -d

    def k_step(t):
        got_k(0, side(t))
        for d in (1, 3, 2):
            k_to_x(side(t), d)
        share(0, side(t), ko, k_c, kc_in)

    def k_rest(t):
        for dx in (1, -1, 2):
            got_k(dx, side(t))
            share(dx, side(t), ko, k_c, kc_in)

    def v_start(dx):
        got_v(dx, 0)
        v_to_z(dx, 0, 1)
        v_to_z(dx, 0, -1)
        share(dx, 0, vo, v_c, vc_in)

    def v_step(t):
        dz = side(t)
        for dx in (0, 1, -1, 2):
            got_v(dx, dz)
            if 0 < dz < NZ // 2:
                v_to_z(dx, dz, -1)
            elif 1 - NZ // 2 < dz < 0:
                v_to_z(dx, dz, 1)
            share(dx, dz, vo, v_c, vc_in)

    def q_step(t):
        h = (lane + t) % NH
        s = y * NH + h
        got_q(0, h)
        for d in (1, 3, 2):
            go(remote(qo.at[s], qo.at[s], q_far, q_in.at[y, h], (x, c, (y + d) % NY, z)))

    def near(t):
        k_step(t)
        q_step(t)

    v_start(0)
    near(0)
    for dx in (1, -1, 2):
        v_start(dx)
    near(1)
    near(2)
    v_step(1)
    v_step(2)
    for t in (3, 4, 5):
        near(t)
    v_step(3)
    v_step(4)
    near(6)
    near(7)
    for t in (0, 1, 2):
        k_rest(t)
    v_step(5)
    v_step(6)
    for t in (3, 4, 5):
        k_rest(t)
    v_step(7)
    k_rest(6)
    k_rest(7)

    def q_rest(i, _):
        got_q(1 + i // NH, i % NH)
        return 0

    lax.fori_loop(0, (NY - 1) * NH, q_rest, 0)
    for sem, count in (
        (kc_in, 32), (vc_in, 32), (q_near, 7), (q_far, 24), (k_z, 7), (k_x, 24), (v_x, 3), (v_z, 28), (k_c, 32), (v_c, 32),
    ):
        some = pl.ds(0, count)
        got(ko, some, sem)


def spread_call(q, k, v):
    vm = pl.BlockSpec(memory_space=pltpu.VMEM)
    held = pl.BlockSpec(memory_space=pltpu.HBM)
    dma = pltpu.SemaphoreType.DMA
    grid = (NX, NZ)
    return pl.pallas_call(
        spread,
        out_shape=(
            jax.ShapeDtypeStruct((NY * NH, RUN, HD), BF16),
            jax.ShapeDtypeStruct((NH * NZ, RUN, HD), BF16),
            jax.ShapeDtypeStruct((NH * NZ, RUN, HD), BF16),
        ),
        in_specs=[held] * 3,
        out_specs=(vm, vm, vm),
        scratch_shapes=[
            dma((NY, NH)), dma(grid), dma(grid), dma, dma, dma, dma, dma, dma, dma, dma, dma, dma,
        ],
        compiler_params=pltpu.CompilerParams(collective_id=1, has_side_effects=True, vmem_limit_bytes=8 << 20),
        name="spread",
    )(q, k, v)


def gather_parts(p_ref, t_ref, o_ref, got, stat, merged, far, near_in, p_in, t_in, p_out, t_out):
    x, c, y, z = here()
    lane = x * NC + c
    mine = pl.ds(pl.multiple_of(lane * HD, HD), HD)

    barrier = pltpu.get_barrier_semaphore()

    def greet(*where):
        pl.semaphore_signal(barrier, 1, device_id=device(*where), device_id_type=pl.DeviceIdType.MESH)

    for d in range(1, NY):
        greet(x, c, (y + d) % NY, z)
    for d in range(1, NH):
        to = (lane + d) % NH
        greet(to // NC, to % NC, y, z)
    pl.semaphore_wait(barrier, NY + NH - 2)

    order = (1, 3, 2, 0)
    for dx in order:
        xx = (x + dx) % NX
        for d in (1, 3, 2):
            yy = (y + d) % NY
            here_ = pl.ds(yy * NH + xx * NC, NC)
            lands = pl.ds(xx * NC, NC)
            remote(p_ref.at[here_], got.at[NY - d, lands], p_out, p_in.at[NY - d, xx], (x, c, yy, z)).start()
            remote(t_ref.at[here_], stat.at[NY - d, lands], t_out, t_in.at[NY - d, xx], (x, c, yy, z)).start()

    for dx in order:
        xx = (x + dx) % NX
        lands = pl.ds(xx * NC, NC)
        for d in (1, 3, 2):
            pltpu.make_async_copy(got.at[d, lands], got.at[d, lands], p_in.at[d, xx]).wait()
            pltpu.make_async_copy(stat.at[d, lands], stat.at[d, lands], t_in.at[d, xx]).wait()
        rows = []
        for cc in range(NC):
            to = xx * NC + cc
            stats = [t_ref[y * NH + to]] + [stat[d, to] for d in range(1, NY)]
            top = functools.reduce(jnp.maximum, [s[2:3] for s in stats])
            shares = [jnp.exp2(s[2:3] - top) * s[0:1] for s in stats]
            whole = functools.reduce(jnp.add, shares)
            rows += [f / whole * (s[1:2] * (1.0 / STEPS)) for f, s in zip(shares, stats)]
        weights = jnp.concatenate(rows + [jnp.zeros((RUN - NC * NY, RUN), F32)], axis=0).T
        for cc in range(NC):
            to = xx * NC + cc
            parts = [p_ref[y * NH + to]] + [got[d, to] for d in range(1, NY)]
            merged[to] = functools.reduce(
                jnp.add,
                [p.astype(jnp.int32).astype(F32) * weights[:, cc * NY + i : cc * NY + i + 1] for i, p in enumerate(parts)],
            )

            def send(to=to, cc=cc):
                remote(merged.at[to], o_ref.at[:, mine], far, near_in.at[lane], (xx, cc, y, z)).start()

            if dx:
                send()
            else:
                pl.when(c != cc)(send)

    o_ref[:, mine] = merged[lane]

    def landed(i, _):
        h = (lane + i) % NH
        cols = o_ref.at[:, pl.ds(pl.multiple_of(h * HD, HD), HD)]
        pltpu.make_async_copy(cols, cols, near_in.at[h]).wait()
        return 0

    lax.fori_loop(1, NH, landed, 0)
    sent = merged.at[pl.ds(0, NH - 1)]
    pltpu.make_async_copy(sent, sent, far).wait()
    for ref, sem in ((p_ref, p_out), (t_ref, t_out)):
        sent = ref.at[pl.ds(0, (NY - 1) * NH)]
        pltpu.make_async_copy(sent, sent, sem).wait()


def gather_call(parts, stats):
    vm = pl.BlockSpec(memory_space=pltpu.VMEM)
    dma = pltpu.SemaphoreType.DMA
    return pl.pallas_call(
        gather_parts,
        out_shape=jax.ShapeDtypeStruct((RUN, NH * HD), F32),
        in_specs=[vm, vm],
        out_specs=vm,
        scratch_shapes=[
            pltpu.VMEM((NY, NH, RUN, HD), jnp.int16), pltpu.VMEM((NY, NH, 8, RUN), F32), pltpu.VMEM((NH, RUN, HD), F32),
            dma, dma((NH,)), dma((NY, NX)), dma((NY, NX)), dma, dma,
        ],
        compiler_params=pltpu.CompilerParams(collective_id=2, has_side_effects=True, vmem_limit_bytes=8 << 20),
        name="gather_parts",
    )(parts, stats)


def on_device(queries, keys, values, positions):
    q, k, v = spread_call(queries, keys, values)
    return gather_call(*attend_call(positions.reshape(-1, RUN), q, k, v, GROUP, REACH))


def solution(mesh):
    finer = Mesh(mesh.devices.reshape(2, NX, NC, 2, NZ), AXES)
    placed = (P(AXES, None), P(AXES, None), P(AXES, None), P())
    return jax.shard_map(on_device, mesh=finer, in_specs=placed, out_specs=P(AXES, None), check_vma=False)
```

time: 614 us -> 587 us (0.956)
  the two profiles are of different devices: /device:TPU:161 before, /device:TPU:19 now
where the time goes in v2:
time: 587 us; the launch traced here: 579 us
  Pallas kernels  575 us (98%)
    pallas_call x1, Pallas kernels, attend_call(): pl.pallas_call(functools.partial(attend, group, reach, n_q, n_k), out_sha...  498 us
    pallas_call x1, Pallas kernels, gather_call(): pl.pallas_call(gather_parts, out_shape=jax.ShapeDtypeStruct((RUN, NH * HD...  44.5 us
    pallas_call x1, Pallas kernels, spread_call(): pl.pallas_call(spread, out_shape=(jax.ShapeDtypeStruct((NY * NH, RUN, HD)...  31.9 us

profile of v2, /device:TPU:19, one launch (start us, length us, event | category | flops | bytes accessed | tf_op | source)
XLA Modules:
  0.0 578.8 jit_solution(2617333911018832775)
XLA Ops:
  0.0 0.0 copy-start
  0.0 0.9 copy-done
  1.0 0.0 copy-start.2
  1.0 0.8 copy-done.2
  1.7 0.0 copy-start.3
  1.7 0.8 copy-done.3
  2.5 31.9 %spread.1 = (bf16[32,128,128]{2,1,0:T(8,128)(2,1)S(1)}, bf16[64,128,128]{2,1,0:T(8,128)(2,1)S(1)}, bf16[64,128,128]{2,1,0:T(8,128)(2,1)S(1)}) custom-call(bf16[128,1024]{1,0:T(8,128)(2,1)S(1)} %copy-done, bf16[128,128]{1,0:T(8,128)(2,1)S(1)} %copy-done.2, bf16[128,128]{1,0:T(8,128)(2,1)S(1)} %copy-done.3), custom_call_target="tpu_custom_call" | custom-call | tf_op jit(solution)/shard_map/spread/pallas_call | solution.py:371
  34.4 0.0 copy-start.1
  34.4 0.9 copy-done.1
  35.3 498.2 %attend.1 = (s16[32,128,128]{2,1,0:T(8,128)(2,1)S(1)}, f32[32,8,128]{2,1,0:T(8,128)S(1)}) custom-call(s32[256,128]{1,0:T(8,128)S(1)} %bitcast.1, bf16[32,128,128]{2,1,0:T(8,128)(2,1)S(1)} %get-tuple-element.10.q_ref, bf16[64,128,128]{2,1,0:T(8,128)(2,1)S(1)} %get-tuple-element.11.k_ref, bf16[64,128,128]{2,1,0:T(8,128)(2,1)S(1)} %get-tuple-element.12.v_ref), custom_call_target="tpu_custom_call" | custom-call | tf_op jit(solution)/shard_map/attend/pallas_call | solution.py:180
  533.5 44.5 %gather_parts.1 = f32[128,1024]{1,0:T(8,128)S(1)} custom-call(s16[32,128,128]{2,1,0:T(8,128)(2,1)S(1)} %get-tuple-element.13.p_ref, f32[32,8,128]{2,1,0:T(8,128)S(1)} %get-tuple-element.14.t_ref), custom_call_target="tpu_custom_call" | custom-call | tf_op jit(solution)/shard_map/gather_parts/pallas_call | solution.py:465
  578.1 0.8 copy.6
Async XLA Ops:
  0.0 0.9 copy-start
  1.0 0.8 copy-start.2
  1.7 0.8 copy-start.3
  34.4 0.9 copy-start.1

commit v3 on v2

--- a/solution.py
+++ b/solution.py
@@ -215,23 +215,24 @@
     )
 
 
-def spread(q_ref, k_ref, v_ref, qo, ko, vo, q_in, k_in, v_in, kc_in, vc_in, q_near, q_far, k_z, k_x, v_x, v_z, k_c, v_c):
+def spread(all_ref, qo, ko, vo, q_in, k_in, v_in, kc_in, vc_in, q_near, q_far, k_z, k_x, v_x, v_z, k_c, v_c):
     x, c, y, z = here()
     lane = x * NC + c
+    k_ref, v_ref = all_ref.at[:, pl.ds(NH * HD, HD)], all_ref.at[:, pl.ds((NH + 1) * HD, HD)]
 
     barrier = pltpu.get_barrier_semaphore()
 
     def greet(*where):
         pl.semaphore_signal(barrier, 1, device_id=device(*where), device_id_type=pl.DeviceIdType.MESH)
 
-    for d in range(1, NZ):
+    for d in (1, NZ - 1):
         greet(x, c, y, (z + d) % NZ)
     for d in range(1, NH):
         to = (lane + d) % NH
         greet(to // NC, to % NC, y, z)
     for d in range(1, NY):
         greet(x, c, (y + d) % NY, z)
-    pl.semaphore_wait(barrier, NZ + NH + NY - 3)
+    pl.semaphore_wait(barrier, NH + NY)
 
     def go(copy):
         copy.start()
@@ -271,12 +272,12 @@
         got(qo, yy * NH + h, q_in.at[yy, h])
 
     def q_cols(h):
-        return q_ref.at[:, pl.ds(pl.multiple_of(h * HD, HD), HD)]
+        return all_ref.at[:, pl.ds(pl.multiple_of(h * HD, HD), HD)]
 
     own_q, own = qo.at[y * NH + lane], slot(0, 0)
     for d in (1, 3, 2):
         go(remote(v_ref, vo.at[own], v_x, v_in.at[x, z], (at_x(d), c, y, z)))
-    for d in (1, NZ - 1, 2, NZ - 2, 3, NZ - 3, 4):
+    for d in (1, -1):
         go(remote(k_ref, ko.at[own], k_z, k_in.at[x, z], (x, c, y, at_z(d))))
     for d in range(1, NH):
         to = (lane + d) % NH
@@ -290,15 +291,21 @@
         return d if t % 2 else -d
 
     def k_step(t):
-        got_k(0, side(t))
+        dz = -side(t)
+        s = slot(0, dz)
+        got_k(0, dz)
+        if -NZ // 2 < dz < 0:
+            go(remote(ko.at[s], ko.at[s], k_z, k_in.at[x, at_z(dz)], (x, c, y, at_z(1))))
+        elif 0 < dz < NZ // 2 - 1:
+            go(remote(ko.at[s], ko.at[s], k_z, k_in.at[x, at_z(dz)], (x, c, y, at_z(-1))))
         for d in (1, 3, 2):
-            k_to_x(side(t), d)
-        share(0, side(t), ko, k_c, kc_in)
+            k_to_x(dz, d)
+        share(0, dz, ko, k_c, kc_in)
 
     def k_rest(t):
         for dx in (1, -1, 2):
-            got_k(dx, side(t))
-            share(dx, side(t), ko, k_c, kc_in)
+            got_k(dx, -side(t))
+            share(dx, -side(t), ko, k_c, kc_in)
 
     def v_start(dx):
         got_v(dx, 0)
@@ -332,24 +339,25 @@
     for dx in (1, -1, 2):
         v_start(dx)
     near(1)
-    near(2)
     v_step(1)
     v_step(2)
-    for t in (3, 4, 5):
-        near(t)
+    near(2)
+    near(3)
     v_step(3)
     v_step(4)
+    near(4)
+    near(5)
+    k_rest(0)
+    k_rest(1)
+    v_step(5)
+    v_step(6)
     near(6)
     near(7)
-    for t in (0, 1, 2):
+    k_rest(2)
+    k_rest(3)
+    v_step(7)
+    for t in (4, 5, 6, 7):
         k_rest(t)
-    v_step(5)
-    v_step(6)
-    for t in (3, 4, 5):
-        k_rest(t)
-    v_step(7)
-    k_rest(6)
-    k_rest(7)
 
     def q_rest(i, _):
         got_q(1 + i // NH, i % NH)
@@ -363,9 +371,9 @@
         got(ko, some, sem)
 
 
-def spread_call(q, k, v):
+def spread_call(together):
     vm = pl.BlockSpec(memory_space=pltpu.VMEM)
-    held = pl.BlockSpec(memory_space=pltpu.HBM)
+    held = pl.BlockSpec(memory_space=pl.ANY)
     dma = pltpu.SemaphoreType.DMA
     grid = (NX, NZ)
     return pl.pallas_call(
@@ -375,14 +383,14 @@
             jax.ShapeDtypeStruct((NH * NZ, RUN, HD), BF16),
             jax.ShapeDtypeStruct((NH * NZ, RUN, HD), BF16),
         ),
-        in_specs=[held] * 3,
+        in_specs=[held],
         out_specs=(vm, vm, vm),
         scratch_shapes=[
             dma((NY, NH)), dma(grid), dma(grid), dma, dma, dma, dma, dma, dma, dma, dma, dma, dma,
         ],
         compiler_params=pltpu.CompilerParams(collective_id=1, has_side_effects=True, vmem_limit_bytes=8 << 20),
         name="spread",
-    )(q, k, v)
+    )(together)
 
 
 def gather_parts(p_ref, t_ref, o_ref, got, stat, merged, far, near_in, p_in, t_in, p_out, t_out):
@@ -477,7 +485,7 @@
 
 
 def on_device(queries, keys, values, positions):
-    q, k, v = spread_call(queries, keys, values)
+    q, k, v = spread_call(jnp.concatenate([queries, keys, values], axis=1))
     return gather_call(*attend_call(positions.reshape(-1, RUN), q, k, v, GROUP, REACH))
 
 

time: 587 us -> 622 us (1.060)
  the two profiles are of different devices: /device:TPU:19 before, /device:TPU:225 now
where the time goes in v3:
time: 622 us; the launch traced here: 621 us
  Pallas kernels  619 us (100%)
    pallas_call x1, Pallas kernels, attend_call(): pl.pallas_call(functools.partial(attend, group, reach, n_q, n_k), out_sha...  535 us
    pallas_call x1, Pallas kernels, gather_call(): pl.pallas_call(gather_parts, out_shape=jax.ShapeDtypeStruct((RUN, NH * HD...  55.2 us
    pallas_call x1, Pallas kernels, spread_call(): pl.pallas_call(spread, out_shape=(jax.ShapeDtypeStruct((NY * NH, RUN, HD)...  28.3 us

profile of v3, /device:TPU:225, one launch (start us, length us, event | category | flops | bytes accessed | tf_op | source)
XLA Modules:
  0.0 621.4 jit_solution(13320137134684915663)
XLA Ops:
  0.0 1.0 pad_maximum_fusion.all_ref
  1.0 28.3 %spread.1 = (bf16[32,128,128]{2,1,0:T(8,128)(2,1)S(1)}, bf16[64,128,128]{2,1,0:T(8,128)(2,1)S(1)}, bf16[64,128,128]{2,1,0:T(8,128)(2,1)S(1)}) custom-call(bf16[128,1280]{1,0:T(8,128)(2,1)S(1)} %pad_maximum_fusion.all_ref), custom_call_target="tpu_custom_call" | custom-call | tf_op jit(solution)/shard_map/spread/pallas_call | solution.py:379
  29.3 0.0 copy-start
  29.3 0.9 copy-done
  30.2 535.2 %attend.1 = (s16[32,128,128]{2,1,0:T(8,128)(2,1)S(1)}, f32[32,8,128]{2,1,0:T(8,128)S(1)}) custom-call(s32[256,128]{1,0:T(8,128)S(1)} %bitcast.1, bf16[32,128,128]{2,1,0:T(8,128)(2,1)S(1)} %get-tuple-element.10.q_ref, bf16[64,128,128]{2,1,0:T(8,128)(2,1)S(1)} %get-tuple-element.11.k_ref, bf16[64,128,128]{2,1,0:T(8,128)(2,1)S(1)} %get-tuple-element.12.v_ref), custom_call_target="tpu_custom_call" | custom-call | tf_op jit(solution)/shard_map/attend/pallas_call | solution.py:180
  565.4 55.2 %gather_parts.1 = f32[128,1024]{1,0:T(8,128)S(1)} custom-call(s16[32,128,128]{2,1,0:T(8,128)(2,1)S(1)} %get-tuple-element.13.p_ref, f32[32,8,128]{2,1,0:T(8,128)S(1)} %get-tuple-element.14.t_ref), custom_call_target="tpu_custom_call" | custom-call | tf_op jit(solution)/shard_map/gather_parts/pallas_call | solution.py:473
  620.6 0.8 copy.6
Async XLA Ops:
  29.3 0.9 copy-start
